TPU v7x, 256 devices: a whole 4x4x8 slice. The times are simulated.
256 devices in a mesh: row: 8 (over x, core), col: 32 (over z, y).
Axes of the slice: x: 4, y: 4, z: 8, core: 2. Of those that a mesh axis runs over, the one named last changes fastest.
Arguments:
- amplitudes: bfloat16 [6144, 73728], P(('row', 'col')), may hold values from -6 to 6
- integrals: bfloat16 [1152, 73728], P('col', 'row'), may hold values from -0.0234375 to 0.0234375
- block_sizes: int32 [8], replicated, may hold values from 57 to 96, as said below
- window_irreps: int32 [2], replicated, may hold values from 0 to 7
Outputs:
- ladder: float32 [6144, 1152], P(('row', 'col'))
Inputs may be any that keep to these rules, and one draw needn't show every extreme that they name: `block_sizes`: each irrep block holds at least 57 orbitals, its first slots; at least one block is full.
All inputs are finite; a program needn't handle non-finite values.
Results may differ from a plain program's by a relative error of at most 0.0003.
Values may be sent and summed in bfloat16 or wider, within the bound.
A program may use at most 128 MiB of HBM per device.

v0:
```python
import jax
import jax.numpy as jnp
from jax import lax
from jax.sharding import PartitionSpec as P

NIRR = 8
NB = 96


def size_lookup(block_sizes, irrep_ids):
    options = jnp.arange(NIRR, dtype=jnp.int32)
    return jnp.sum(
        jnp.where(irrep_ids[:, None] == options[None, :], block_sizes[None, :], 0), axis=1
    )


def live_columns(block_sizes, pair_irrep, offset, count):
    pair_index = offset + jnp.arange(count, dtype=jnp.int32)
    irrep_c = pair_index // (NB * NB)
    slot_c = pair_index // NB % NB
    slot_d = pair_index % NB
    irrep_d = jnp.bitwise_xor(irrep_c, pair_irrep)
    live_mask = (slot_c < size_lookup(block_sizes, irrep_c)) & (
        slot_d < size_lookup(block_sizes, irrep_d)
    )
    return live_mask.astype(jnp.bfloat16)


def contract(left_rows, right_rows):
    return lax.dot_general(
        left_rows, right_rows, (((1,), (1,)), ((), ())), preferred_element_type=jnp.float32
    )


def shards(amplitudes, integrals, block_sizes, window_irreps):
    n_col = lax.axis_size("col")
    local_width = integrals.shape[1]
    window_rows = integrals.shape[0] * n_col
    transposed = lax.all_to_all(amplitudes, "row", split_axis=1, concat_axis=0, tiled=True)
    offset = lax.axis_index("row") * local_width
    live_mask = live_columns(block_sizes, window_irreps[0], offset, local_width)
    masked = transposed * live_mask[None, :]
    partial_sum = contract(masked, lax.all_gather(integrals, "col", axis=0, tiled=True))
    ladder = lax.psum_scatter(partial_sum, "row", scatter_dimension=0, tiled=True)
    size_b = jnp.sum(
        jnp.where(jnp.arange(NIRR, dtype=jnp.int32) == window_irreps[1], block_sizes, 0)
    )
    slot_mask = jnp.arange(window_rows, dtype=jnp.int32) % NB < size_b
    return jnp.where(slot_mask[None, :], ladder, jnp.float32(0.0))


def solution(mesh):
    placed = (P(("row", "col"), None), P("col", "row"), P(), P())
    return jax.shard_map(
        shards, mesh=mesh, in_specs=placed, out_specs=P(("row", "col"), None), check_vma=False
    )
```

profile of v0, /device:TPU:1, one launch (start us, length us, event | category | flops | bytes accessed | tf_op | source)
XLA Modules:
  0.0 260.3 jit_solution(1216563806489351661)
XLA Ops:
  6.5 0.0 all-gather.3.cloned.1.call-start
  6.5 0.7 all-gather.3.cloned.1.call-update
  7.3 4.0 %copy.10 = bf16[3,8,8,9216]{3,2,0,1:T(8,128)(2,1)} copy(bf16[3,8,8,9216]{3,2,1,0:T(8,128)(2,1)} %bitcast.14) | data formatting | bytes 7077888 | tf_op jit(solution)/shard_map/all_to_all | solution.py:39
  11.3 0.0 copy-start.1
  11.3 0.0 copy-start.2
  11.3 6.9 %all-to-all-start = ((bf16[24,8,9216]{2,0,1:T(8,128)(2,1)}), bf16[24,8,9216]{2,0,1:T(8,128)(2,1)S(1)}, u32[]{:S(2)}, u32[]{:S(2)}) async-start(bf16[24,8,9216]{2,0,1:T(8,128)(2,1)} %bitcast.13), calls=%async_computation | async-start | bytes 7077888 | tf_op jit(solution)/shard_map/all_to_all | solution.py:39
  18.2 0.0 reduce-scatter.4.cloned.1.call-start
  18.3 0.0 copy-done.1
  18.3 0.6 fusion.15
  18.9 0.7 add_select_fusion.1
  19.5 0.0 copy-done.2
  19.6 0.3 select_reduce_fusion
  19.8 0.7 fusion.9
  20.5 39.5 %all-to-all-done = bf16[24,8,9216]{2,0,1:T(8,128)(2,1)S(1)} async-done(((bf16[24,8,9216]{2,0,1:T(8,128)(2,1)}), bf16[24,8,9216]{2,0,1:T(8,128)(2,1)S(1)}, u32[]{:S(2)}, u32[]{:S(2)}) %all-to-all-start) | async-done | bytes 3538976 | tf_op jit(solution)/shard_map/all_to_all | solution.py:39
  60.1 2.9 %bitcast_multiply_fusion = bf16[192,9216]{1,0:T(8,128)(2,1)} fusion(bf16[24,8,9216]{2,0,1:T(8,128)(2,1)S(1)} %all-to-all-done, bf16[9216]{0:T(1024)(128)(2,1)} %fusion.9), kind=kLoop, calls=%fused_computation.1 | loop fusion | flops 1769472 | bytes 7096320 | tf_op jit(solution)/shard_map/mul | solution.py:42
  62.9 125.5 %all-gather.3.cloned.1.call-done = bf16[32,36,9216]{2,1,0:T(8,128)(2,1)} async-done(((bf16[1,36,9216]{2,1,0:T(8,128)(2,1)}), bf16[32,36,9216]{2,1,0:T(8,128)(2,1)}) %all-gather.3.cloned.1.call-update) | async-done | bytes 21233680 | tf_op jit(solution)/shard_map/all_gather | solution.py:43
  188.4 22.0 %reshape.60 = bf16[1152,9216]{1,0:T(8,128)(2,1)} reshape(bf16[32,36,9216]{2,1,0:T(8,128)(2,1)} %all-gather.3.cloned.1.call-done) | data formatting | bytes 42467328
  210.4 0.0 copy-done
  210.4 12.1 %fusion.16 = f32[192,1152]{1,0:T(8,128)} fusion(bf16[192,9216]{1,0:T(8,128)(2,1)S(1)} %copy-done, bf16[1152,9216]{1,0:T(8,128)(2,1)} %reshape.60), kind=kOutput, calls=%fused_computation.34 | convolution fusion | flops 4076863488 | bytes 25657344 | tf_op jit(solution)/shard_map/dot_general | solution.py:30
  222.5 0.0 reduce-scatter.4.cloned.1.call-update
  222.6 1.3 fusion.14
  223.8 0.7 fusion.10
  224.5 27.4 %reduce-scatter.4.cloned.1.call-done = f32[24,1152]{1,0:T(8,128)} async-done(((f32[192,1152]{1,0:T(8,128)}), f32[24,1152]{1,0:T(8,128)}) %reduce-scatter.4.cloned.1.call-update) | async-done | bytes 110608
  251.9 1.6 broadcast_select_fusion
  (1 shorter events, 0.0 us)
Async XLA Ops:
  6.5 181.9 %all-gather.3.cloned.1.call-start = ((), (), s32[]{:S(2)}) async-start(), calls=%async_computation.2 | async-start | bytes 24330240 | tf_op jit(solution)/shard_map/all_gather | solution.py:43
  11.3 6.9 %copy-start.1 = (s32[2]{0:T(128)S(1)}, s32[2]{0:T(128)}, u32[]{:S(2)}) copy-start(s32[2]{0:T(128)} %param.7) | copy-start | bytes 28
  11.3 8.2 %copy-start.2 = (s32[8]{0:T(128)S(1)}, s32[8]{0:T(128)}, u32[]{:S(2)}) copy-start(s32[8]{0:T(128)} %param.6) | copy-start | bytes 100
  11.3 48.7 %all-to-all-start = ((bf16[24,8,9216]{2,0,1:T(8,128)(2,1)}), bf16[24,8,9216]{2,0,1:T(8,128)(2,1)S(1)}, u32[]{:S(2)}, u32[]{:S(2)}) async-start(bf16[24,8,9216]{2,0,1:T(8,128)(2,1)} %bitcast.13), calls=%async_computation | async-start | bytes 7077888 | tf_op jit(solution)/shard_map/all_to_all | solution.py:39
  18.2 233.6 %reduce-scatter.4.cloned.1.call-start = ((), (), s32[]{:S(2)}) async-start(), calls=%async_computation.3 | async-start | bytes 995328
  62.9 147.5 %copy-start = (bf16[192,9216]{1,0:T(8,128)(2,1)S(1)}, bf16[192,9216]{1,0:T(8,128)(2,1)}, u32[]{:S(2)}) copy-start(bf16[192,9216]{1,0:T(8,128)(2,1)} %bitcast_multiply_fusion) | copy-start | bytes 10616836
Sparse Core Ops, SparseCore 0:
  9.9 178.4 all-gather.2
  222.7 29.1 reduce-scatter.3
where the time goes:
time: 263 us; the launch traced here: 260 us
  waiting for transfers between devices  193 us (73%)
  local copies, waits for them, and re-layouts  26.6 us (10%)
  between operations  13.4 us (5%)
  matrix products  12.1 us (5%)
  other arithmetic  7.95 us (3%)
  starting transfers between devices  6.94 us (3%)
    all_gather x1, waiting for transfers between devices, shards(): lax.all_gather(integrals, 'col', axis=0, tiled=True)  126 us
    all_to_all x1, waiting for transfers between devices, shards(): lax.all_to_all(amplitudes, 'row', split_axis=1, concat_axis=0, tiled=True)  39.5 us
    unnamed x3, waiting for transfers between devices  28.1 us
    unnamed x7, local copies, waits for them, and re-layouts  22 us
    dot_general x1, matrix products, contract(): lax.dot_general(left_rows, right_rows, (((1,), (1,)), ((), ())), preferre...  12.1 us
    all_to_all x1, starting transfers between devices, shards(): lax.all_to_all(amplitudes, 'row', split_axis=1, concat_axis=0, tiled=True)  6.94 us
  transfers between devices with their start and end apart: 3, of which 3 were waited for; matrix products, arithmetic and copies ran while one was open for 4% of the time, Pallas kernels for 0%

commit v1 on v0

v1 whole, which is shorter than its diff:
```python
import functools

import jax
import jax.numpy as jnp
from jax import lax
from jax.experimental import pallas as pl
from jax.experimental.pallas import tpu as pltpu
from jax.sharding import PartitionSpec as P

NIRR = 8
NB = 96
MESH = pl.DeviceIdType.MESH
LANES = 128
QUAD = 4 * NB
NQ = 24
WT = 5
KT = 18
UNROLL = 6
SPARE = 24
PEERS = [(1, 0), (0, 1), (3, 0), (0, 3), (2, 0), (0, 2), (1, 1), (3, 3), (1, 3), (3, 1),
         (2, 1), (1, 2), (2, 3), (3, 2), (2, 2)]


def selection(size):
    i = lax.broadcasted_iota(jnp.int32, (QUAD, QUAD), 0)
    k = (i >= NB).astype(jnp.int32) + (i >= 2 * NB).astype(jnp.int32) + (i >= 3 * NB).astype(jnp.int32)
    d = i - NB * k
    target = jnp.where(d < size, k * size + d, -1)
    j = lax.broadcasted_iota(jnp.int32, (QUAD, QUAD), 1)
    return jnp.where(j == target, 1.0, 0.0).astype(jnp.bfloat16)


def moved(first, second, following, lane, shift, rest):
    run = pltpu.roll(jnp.where(lane >= shift, first, second), (LANES - shift) & 127, 1)
    return jnp.where(lane < rest, run, pltpu.roll(following, rest & 127, 1))


def tile_at(t):
    return pl.ds(pl.multiple_of(t * LANES, LANES), LANES)


def pack_kernel(sizes, window, a_hbm, b_hbm, a_out, b_out, place, width,
                a_v, b_v, y_a, x_b, y_b, a_pack, b_pack, s_load, s_store):
    row, col = lax.axis_index("row"), lax.axis_index("col")
    core, chip = row % 2, (row // 2) * 4 + col % 4
    load_b = pltpu.make_async_copy(b_hbm, b_v, s_load.at[8])
    load_b.start()
    loads = []
    for h in range(NIRR):
        part = pl.ds(h * NB * NB, NB * NB)
        loads.append(pltpu.make_async_copy(a_hbm.at[:, part], a_v.at[:, part], s_load.at[h]))
        loads[-1].start()
    g = window[0]

    def irrep(h):
        size = sizes[h ^ g]
        live = sizes[h] * size
        return size, live, (live + LANES - 1) // LANES

    base, total = [], [0, 0]
    for h in range(NIRR):
        base.append(total[h % 2])
        total[h % 2] = total[h % 2] + irrep(h)[2]
    width[0] = jnp.maximum(total[0] + 15, total[1] + 15) // 16
    mine = 0
    for h in range(NIRR):
        mine = jnp.where(row == h, base[h], mine)
    ends = jnp.where(core == 0, total[0], total[1])

    @pl.loop(0, KT)
    def _(i):
        n = 16 * i + chip
        which, start = jnp.int32(0), jnp.int32(0)
        for k in range(1, 4):
            first = jnp.where(core == 0, base[2 * k], base[2 * k + 1])
            which = jnp.where(n >= first, k, which)
            start = jnp.where(n >= first, first, start)
        place[0, i] = which
        place[1, i] = jnp.minimum((n - start) // 16, WT - 1)
        place[2, i] = (n < ends).astype(jnp.int32)

    def step(quad, offset, quad_width):
        offset = offset + LANES
        over = offset >= quad_width
        return jnp.where(over, quad + 1, quad), jnp.where(over, offset - quad_width, offset)

    load_b.wait()
    for q in range(NQ):
        x_b[q, 0:36, :] = b_v[:, q * QUAD:(q + 1) * QUAD].astype(jnp.float32)
    size, live, _ = irrep(row)
    y_b[3 * NQ] = jnp.zeros((40, LANES), jnp.float32)
    packed_b = jnp.dot(
        x_b[...].reshape(NQ * 40, QUAD).astype(jnp.bfloat16), selection(size),
        preferred_element_type=jnp.float32)
    for q in range(NQ):
        for t in range(3):
            y_b[3 * q + t] = packed_b[40 * q:40 * q + 40, t * LANES:(t + 1) * LANES]
    lane_b = lax.broadcasted_iota(jnp.int32, (40, LANES), 1)

    @pl.loop(0, 16 * WT // 8, init_carry=(jnp.int32(0), jnp.int32(0)))
    def _(group, carry):
        quad, offset = carry
        for u in range(8):
            m = 8 * group + u
            t = jnp.minimum(3 * quad + offset // LANES, 3 * NQ - 1)
            after = jnp.minimum(3 * quad + 3, 3 * NQ)
            v = moved(y_b[t], y_b[t + 1], y_b[after], lane_b, offset % LANES, 4 * size - offset)
            b_pack[(mine + m) % 16, m // 16] = jnp.where(lane_b < live - m * LANES, v, 0.0).astype(jnp.bfloat16)
            quad, offset = step(quad, offset, 4 * size)
        return quad, offset

    stores = [pltpu.make_async_copy(b_pack, b_out, s_store.at[2])]
    stores[0].start()

    for t in range(SPARE):
        y_a[NIRR * NQ * 3 + t] = jnp.zeros((24, LANES), jnp.float32)
    for h in range(NIRR):
        loads[h].wait()

    @pl.loop(0, NIRR)
    def _(h):
        wide = [a_v[:, pl.ds(pl.multiple_of(h * NB * NB + q * QUAD, LANES), QUAD)].astype(jnp.float32)
                for q in range(NQ)]
        packed = jnp.dot(jnp.concatenate(wide, axis=0).astype(jnp.bfloat16), selection(irrep(h)[0]),
                         preferred_element_type=jnp.float32)
        for q in range(NQ):
            for t in range(3):
                y_a[(h * NQ + q) * 3 + t] = packed[24 * q:24 * q + 24, t * LANES:(t + 1) * LANES]

    lane_a = lax.broadcasted_iota(jnp.int32, (24, LANES), 1)
    for half in range(2):
        @pl.loop(0, 4, init_carry=jnp.int32(0))
        def _(k, first):
            h = 2 * k + half
            size, _, count = irrep(h)

            @pl.loop(0, (count + UNROLL - 1) // UNROLL, init_carry=(h * NQ, jnp.int32(0)))
            def _(group, carry):
                quad, offset = carry
                for u in range(UNROLL):
                    n = first + UNROLL * group + u
                    t = 3 * quad + offset // LANES
                    v = moved(y_a[t], y_a[t + 1], y_a[3 * quad + 3], lane_a, offset % LANES, 4 * size - offset)
                    a_pack[half, n % 16, :, tile_at(n // 16)] = v.astype(jnp.bfloat16)
                    quad, offset = step(quad, offset, 4 * size)
                return quad, offset

            return first + count

        @pl.loop(total[half], 16 * KT)
        def _(n):
            a_pack[half, n % 16, :, tile_at(n // 16)] = jnp.zeros((24, LANES), jnp.bfloat16)

        stores.append(pltpu.make_async_copy(a_pack.at[half, :, :, 0:KT * LANES], a_out.at[half], s_store.at[half]))
        stores[-1].start()
    for c in stores:
        c.wait()


def pack_call(sizes, window, amplitudes, integrals):
    bf, f32 = jnp.bfloat16, jnp.float32
    smem = pl.BlockSpec(memory_space=pltpu.SMEM)
    hbm = pl.BlockSpec(memory_space=pl.ANY)
    return pl.pallas_call(
        pack_kernel,
        out_shape=(jax.ShapeDtypeStruct((2, 16, 24, KT * LANES), bf), jax.ShapeDtypeStruct((16, WT, 40, LANES), bf),
                   jax.ShapeDtypeStruct((3, KT), jnp.int32), jax.ShapeDtypeStruct((1,), jnp.int32)),
        in_specs=[smem, smem, hbm, hbm],
        out_specs=(hbm, hbm, smem, smem),
        scratch_shapes=[
            pltpu.VMEM((24, NIRR * NB * NB), bf),
            pltpu.VMEM((36, NB * NB), bf),
            pltpu.VMEM((NIRR * NQ * 3 + SPARE, 24, LANES), f32),
            pltpu.VMEM((NQ, 40, QUAD), f32),
            pltpu.VMEM((NQ * 3 + 1, 40, LANES), f32),
            pltpu.VMEM((2, 16, 24, (KT + 1) * LANES), bf),
            pltpu.VMEM((16, WT, 40, LANES), bf),
            pltpu.SemaphoreType.DMA((9,)), pltpu.SemaphoreType.DMA((3,)),
        ],
        compiler_params=pltpu.CompilerParams(vmem_limit_bytes=60 * 2**20),
    )(sizes, window, amplitudes, integrals)


def kernel(kt, place, window, sizes, a_hbm, b_hbm, o_ref,
           b_recv, dense, a_recv, a_mat, b_main, b_rest, c_part, c_in1, c_sum, c_in2, c_out,
           s_own, s_bs, s_br, s_as, s_ar, s_zs, s_zr, s_rs, s_rr, s_ks, s_kr, s_c1s, s_c1r, s_c2s, s_c2r):
    row, col = lax.axis_index("row"), lax.axis_index("col")
    x, core = row // 2, row % 2
    z, y = col // 4, col % 4
    chip = x * 4 + y

    def plane(dx, dy):
        px, py = (x + dx) % 4, (y + dy) % 4
        return (px * 2 + core, z * 4 + py), px * 4 + py

    up = (row, ((z + 1) % 8) * 4 + y)
    down = (row, ((z + 7) % 8) * 4 + y)
    sibling = (x * 2 + 1 - core, col)

    used = pl.ds(0, kt * LANES)
    own = [pltpu.make_async_copy(b_hbm.at[chip], b_recv.at[chip], s_own.at[0])]
    for half in range(2):
        own.append(pltpu.make_async_copy(a_hbm.at[half, chip, :, used], a_recv.at[half, chip], s_own.at[1 + half]))
    for c in own:
        c.start()

    barrier = pltpu.get_barrier_semaphore()
    for who in [plane(*p)[0] for p in PEERS] + [up, down, sibling]:
        pl.semaphore_signal(barrier, 1, device_id=who, device_id_type=MESH)
    pl.semaphore_wait(barrier, len(PEERS) + 3)

    def remote(src, dst, send, recv, who):
        return pltpu.make_async_remote_copy(src, dst, send, recv, device_id=who, device_id_type=MESH)

    b_copies, a_copies = [], [[], []]
    for i, (dx, dy) in enumerate(PEERS):
        who, target = plane(dx, dy)
        b_copies.append(remote(b_hbm.at[target], b_recv.at[chip], s_bs.at[i], s_br.at[i], who))
        b_copies[-1].start()
    for half in range(2):
        for i, (dx, dy) in enumerate(PEERS):
            who, target = plane(dx, dy)
            a_copies[half].append(remote(a_hbm.at[half, target, :, used], a_recv.at[half, chip],
                                         s_as.at[half, i], s_ar.at[half, i], who))
            a_copies[half][-1].start()
    for c in own:
        c.wait()

    for c in b_copies:
        c.wait()

    @pl.loop(0, kt)
    def _(i):
        px, k, valid = place[0, i], place[1, i], place[2, i]
        for py in range(4):
            v = b_recv[px * 4 + py, k].astype(jnp.float32)
            dense[36 * py:36 * py + 36, :] = jnp.where(valid > 0, v, 0.0)[0:36, :]
        d = dense[...].astype(jnp.bfloat16)
        b_main[0, core, :, tile_at(i)] = d[0:128]
        b_rest[core, pl.ds(pl.multiple_of(16 * z, 16), 16), tile_at(i)] = d[128:144]

    def main_copies(step):
        rows_up = pl.ds(0, 128) if step < 3 else pl.ds(0, 64)
        rows_down = pl.ds(0, 128) if step < 3 else pl.ds(64, 64)
        a, b = (8 - step) % 8, (7 - step) % 8
        return (remote(b_main.at[a, core, rows_up], b_main.at[b, core, rows_up],
                       s_zs.at[0, step], s_zr.at[0, step], up),
                remote(b_main.at[step, core, rows_down], b_main.at[step + 1, core, rows_down],
                       s_zs.at[1, step], s_zr.at[1, step], down))

    def rest_copies(step):
        at_up = pl.ds(pl.multiple_of(16 * ((z + 8 - step) % 8), 16), 16)
        at_down = pl.ds(pl.multiple_of(16 * ((z + step) % 8), 16), 16)
        out = [remote(b_rest.at[core, at_up], b_rest.at[core, at_up], s_rs.at[0, step], s_rr.at[0, step], up)]
        if step < 3:
            out.append(remote(b_rest.at[core, at_down], b_rest.at[core, at_down],
                              s_rs.at[1, step], s_rr.at[1, step], down))
        return out

    def share(r):
        return remote(b_main.at[r, core], b_main.at[r, core], s_ks.at[r], s_kr.at[r], sibling)

    def start(copies):
        for c in copies:
            c.start()
        return copies

    def got(copies):
        for c in copies:
            c.wait_recv()

    main, rest, shared = [], [], {}
    rest.append(start(rest_copies(0)))
    main.append(start(main_copies(0)))
    shared[0] = share(0)
    shared[0].start()

    def next_rest(step):
        got(rest[step - 1])
        rest.append(start(rest_copies(step)))

    def next_main(step):
        got(main[step - 1])
        main.append(start(main_copies(step)))
        for r in (step, 8 - step):
            shared[r] = share(r)
            shared[r].start()

    def repack(half):
        got(a_copies[half])

        @pl.loop(0, 8)
        def _(s):
            v = a_recv[half, pl.ds(2 * s, 2)].astype(jnp.float32)
            a_mat[half, pl.ds(pl.multiple_of(48 * s, 48), 48), :] = v.reshape(48, kt * LANES).astype(jnp.bfloat16)

    next_rest(1)
    next_rest(2)
    next_rest(3)
    next_main(1)
    repack(0)
    next_main(2)
    next_main(3)
    repack(1)
    got(rest[3])
    share_rest = remote(b_rest.at[core], b_rest.at[core], s_ks.at[8], s_kr.at[8], sibling)
    share_rest.start()

    def product(r):
        total = None
        for half in range(2):
            right = b_main[r, half] if r < 8 else b_rest[half]
            v = lax.dot_general(a_mat[half], right, (((1,), (1,)), ((), ())), preferred_element_type=jnp.float32)
            total = v if total is None else total + v
        c_part[r] = total.reshape(4, 4, 24, LANES)

    first, second = {}, {}

    def line(r, k, phase):
        along_x = (r % 2 == 0) == (phase == 1)
        return plane(k, 0)[0] if along_x else plane(0, k)[0]

    def send_first(r):
        first[r] = []
        for k in (1, 3, 2):
            if r % 2 == 0:
                src = c_part.at[r, (x + k) % 4]
            else:
                src = c_part.at[r, :, (y + k) % 4]
            first[r].append(remote(src, c_in1.at[r, k - 1], s_c1s.at[r, k - 1], s_c1r.at[r, k - 1], line(r, k, 1)))
        start(first[r])

    def send_second(r):
        got(first[r])
        own = c_part[r, x] if r % 2 == 0 else c_part[r, :, y]
        c_sum[r] = own + c_in1[r, 0] + c_in1[r, 1] + c_in1[r, 2]
        second[r] = []
        for k in (1, 3, 2):
            src = c_sum.at[r, (y + k) % 4] if r % 2 == 0 else c_sum.at[r, (x + k) % 4]
            second[r].append(remote(src, c_in2.at[r, k - 1], s_c2s.at[r, k - 1], s_c2r.at[r, k - 1], line(r, k, 2)))
        start(second[r])

    def finish(r):
        got(second[r])
        own = c_sum[r, y] if r % 2 == 0 else c_sum[r, x]
        at = (z + r) % 8 if r < 8 else 8
        c_out[at] = own + c_in2[r, 0] + c_in2[r, 1] + c_in2[r, 2]

    def tile(r):
        if r < 8:
            shared[r].wait_recv()
        else:
            share_rest.wait_recv()
        product(r)
        send_first(r)

    for r in (0, 1, 7, 2, 6):
        tile(r)
    tile(8)
    for r in (3, 5):
        tile(r)
    for r in (0, 1, 7, 2, 6, 8):
        send_second(r)
    got(main[3])
    shared[4] = share(4)
    shared[4].start()
    tile(4)
    for r in (3, 5):
        send_second(r)
    for r in (0, 1, 7, 2, 6, 8):
        finish(r)
    send_second(4)
    for r in (3, 5, 4):
        finish(r)
    size_b = jnp.int32(0)
    for h in range(NIRR):
        size_b = jnp.where(window[1] == h, sizes[h], size_b)
    for t in range(8):
        o_ref[:, 144 * t:144 * t + 128] = c_out[t]
        o_ref[:, 144 * t + 128:144 * t + 144] = c_out[8, :, 16 * t:16 * t + 16]
    slot = lax.broadcasted_iota(jnp.int32, (24, 8 * 144), 1)
    o_ref[...] = jnp.where(slot % NB < size_b, o_ref[...], 0.0)
    for group in rest + main + a_copies + list(first.values()) + list(second.values()):
        for c in group:
            c.wait_send()
    for c in list(shared.values()) + [share_rest]:
        c.wait_send()


def ladder_call(kt, collective_id, place, window, sizes, a_packed, b_packed):
    kh = kt * LANES
    bf, f32 = jnp.bfloat16, jnp.float32
    dma = pltpu.SemaphoreType.DMA
    smem = pl.BlockSpec(memory_space=pltpu.SMEM)
    hbm = pl.BlockSpec(memory_space=pl.ANY)
    return pl.pallas_call(
        functools.partial(kernel, kt),
        out_shape=jax.ShapeDtypeStruct((24, 8 * 144), f32),
        in_specs=[smem] * 3 + [hbm] * 2,
        out_specs=pl.BlockSpec(memory_space=pltpu.VMEM),
        scratch_shapes=[
            pltpu.VMEM((16, WT, 40, LANES), bf),
            pltpu.VMEM((144, LANES), f32),
            pltpu.VMEM((2, 16, 24, kh), bf),
            pltpu.VMEM((2, 384, kh), bf),
            pltpu.VMEM((8, 2, 128, kh), bf),
            pltpu.VMEM((2, 128, kh), bf),
            pltpu.VMEM((9, 4, 4, 24, LANES), f32),
            pltpu.VMEM((9, 3, 4, 24, LANES), f32),
            pltpu.VMEM((9, 4, 24, LANES), f32),
            pltpu.VMEM((9, 3, 24, LANES), f32),
            pltpu.VMEM((9, 24, LANES), f32),
            dma((3,)), dma((15,)), dma((15,)), dma((2, 15)), dma((2, 15)),
            dma((2, 4)), dma((2, 4)), dma((2, 4)), dma((2, 4)), dma((9,)), dma((9,)),
            dma((9, 3)), dma((9, 3)), dma((9, 3)), dma((9, 3)),
        ],
        compiler_params=pltpu.CompilerParams(
            collective_id=collective_id, has_side_effects=True, vmem_limit_bytes=60 * 2**20),
    )(place, window, sizes, a_packed, b_packed)


def shards(amplitudes, integrals, block_sizes, window_irreps):
    a_packed, b_packed, place, width = pack_call(block_sizes, window_irreps, amplitudes, integrals)
    return ladder_call(KT, 0, place, window_irreps, block_sizes, a_packed, b_packed)


def solution(mesh):
    placed = (P(("row", "col"), None), P("col", "row"), P(), P())
    return jax.shard_map(
        shards, mesh=mesh, in_specs=placed, out_specs=P(("row", "col"), None), check_vma=False
    )
```

time: 263 us -> 127 us (0.48)
  waiting for transfers between devices: 193 us -> 0 us
  Pallas kernels: 0 us -> 125 us
  local copies, waits for them, and re-layouts: 26.6 us -> 1.55 us
  between operations: 13.4 us -> 0.02 us
  matrix products: 12.1 us -> 0 us
  other arithmetic: 7.95 us -> 0 us
  starting transfers between devices: 6.94 us -> 0 us
    all_gather x1 -> x0, waiting for transfers between devices: 126 us -> none  [shards(): lax.all_gather(integrals, 'col', axis=0, tiled=True)]
    pallas_call x0 -> x2, Pallas kernels: none -> 125 us  [the longest x1 105 us: ladder_call(): pl.pallas_call(functools.partial(kernel, kt), out_shape=jax.ShapeDtypeStr...]
    all_to_all x1 -> x0, waiting for transfers between devices: 39.5 us -> none  [shards(): lax.all_to_all(amplitudes, 'row', split_axis=1, concat_axis=0, tiled=True)]
    unnamed x3 -> x0, waiting for transfers between devices: 28.1 us -> none
    unnamed x7 -> x1, local copies, waits for them, and re-layouts: 22 us -> 1.55 us
    dot_general x1 -> x0, matrix products: 12.1 us -> none  [contract(): lax.dot_general(left_rows, right_rows, (((1,), (1,)), ((), ())), preferre...]
    all_to_all x1 -> x0, starting transfers between devices: 6.94 us -> none  [shards(): lax.all_to_all(amplitudes, 'row', split_axis=1, concat_axis=0, tiled=True)]
    all_to_all x1 -> x0, local copies, waits for them, and re-layouts: 4.05 us -> none  [shards(): lax.all_to_all(amplitudes, 'row', split_axis=1, concat_axis=0, tiled=True)]
  transfers between devices with their start and end apart: 3 -> 0, of which waited for: 3 -> 0; matrix products, arithmetic and copies ran while one was open for 4% -> 0% of each run, Pallas kernels for 0% -> 0%
where the time goes in v1:
time: 127 us
  Pallas kernels  125 us (98%)
  local copies, waits for them, and re-layouts  1.55 us (1%)
    pallas_call x1, Pallas kernels, ladder_call(): pl.pallas_call(functools.partial(kernel, kt), out_shape=jax.ShapeDtypeStr...  105 us
    pallas_call x1, Pallas kernels, pack_call(): pl.pallas_call(pack_kernel, out_shape=(jax.ShapeDtypeStruct((2, 16, 24, K...  20.7 us

profile of v1, /device:TPU:1, one launch (start us, length us, event | category | flops | bytes accessed | tf_op | source)
XLA Modules:
  0.0 126.9 jit_solution(7539029748416629318)
XLA Ops:
  0.0 20.7 %shard_map.46 = (bf16[2,16,24,2304]{3,2,1,0:T(8,128)(2,1)}, bf16[16,5,40,128]{3,2,1,0:T(8,128)(2,1)}, s32[3,18]{1,0:T(4,128)}, s32[1]{0:T(128)}) custom-call(s32[8]{0:T(128)} %sizes.3, s32[2]{0:T(128)} %window.3, bf16[24,73728]{1,0:T(8,128)(2,1)} %a_hbm.1, bf16[36,9216]{1,0:T(8,128)(2,1)} %b_hbm.1), custom_call_target="tpu_custom_call" | custom-call | tf_op jit(solution)/shard_map/pallas_call | solution.py:164
  20.7 104.7 %shard_map.47 = f32[24,1152]{1,0:T(8,128)} custom-call(s32[3,18]{1,0:T(4,128)} %get-tuple-element.8.place, s32[2]{0:T(128)} %window.3, s32[8]{0:T(128)} %sizes.3, bf16[2,16,24,2304]{3,2,1,0:T(8,128)(2,1)} %get-tuple-element.9.a_hbm, bf16[16,5,40,128]{3,2,1,0:T(8,128)(2,1)} %get-tuple-element.10.b_hbm), custom_call_target="tpu_custom_call" | custom-call | tf_op jit(solution)/shard_map/pallas_call | solution.py:396
  125.3 1.5 %copy.6 = f32[24,1152]{1,0:T(8,128)} copy(f32[24,1152]{1,0:T(8,128)} %shard_map.47) | data formatting | bytes 221184

commit v2 on v0

v2 whole, which is shorter than its diff:
```python
import functools

import jax
import jax.numpy as jnp
from jax import lax
from jax.experimental import pallas as pl
from jax.experimental.pallas import tpu as pltpu
from jax.sharding import PartitionSpec as P

NIRR = 8
NB = 96
MESH = pl.DeviceIdType.MESH
LANES = 128
QUAD = 4 * NB
NQ = 24
WT = 5
KT = 18
EARLY = 2
FIELDS = 5
WIDTHS = (12, 13, 15, 18)

def selection(size):
    i = lax.broadcasted_iota(jnp.int32, (QUAD, QUAD), 0)
    k = (i >= NB).astype(jnp.int32) + (i >= 2 * NB).astype(jnp.int32) + (i >= 3 * NB).astype(jnp.int32)
    d = i - NB * k
    target = jnp.where(d < size, k * size + d, -1)
    j = lax.broadcasted_iota(jnp.int32, (QUAD, QUAD), 1)
    return jnp.where(j == target, 1.0, 0.0).astype(jnp.bfloat16)


def moved(first, second, following, lane, shift, rest):
    run = pltpu.roll(jnp.where(lane >= shift, first, second), (LANES - shift) & 127, 1)
    return jnp.where(lane < rest, run, pltpu.roll(following, rest & 127, 1))


def tile_at(t):
    return pl.ds(pl.multiple_of(t * LANES, LANES), LANES)


def deal_kernel(sizes, window, b_hbm, b_out, table, width, b_v, x_b, y_b, b_pack, s_load):
    row = lax.axis_index("row")
    load_b = pltpu.make_async_copy(b_hbm, b_v, s_load)
    load_b.start()
    g = window[0]
    size = [sizes[h ^ g] for h in range(NIRR)]
    live = [sizes[h] * size[h] for h in range(NIRR)]
    tiles = [(live[h] + LANES - 1) // LANES for h in range(NIRR)]
    full = [jnp.maximum(tiles[h] // 16, EARLY) for h in range(NIRR)]
    left = [jnp.maximum(tiles[h] - 16 * full[h], 0) for h in range(NIRR)]
    start = [None] * NIRR
    all_full, all_left = [0, 0], [0, 0]
    for h in range(NIRR):
        start[h] = all_left[h % 2]
        all_full[h % 2] = all_full[h % 2] + full[h]
        all_left[h % 2] = all_left[h % 2] + left[h]
    slots = [all_full[p] + (all_left[p] + 15) // 16 for p in range(2)]
    width[0] = jnp.maximum(slots[0], slots[1])

    line = lax.broadcasted_iota(jnp.int32, (8, LANES), 0)
    lane = lax.broadcasted_iota(jnp.int32, (8, LANES), 1)
    fields = [jnp.zeros((8, LANES), jnp.int32)] * FIELDS
    for half in range(2):
        entry = (line - 3 * half) * LANES + lane
        slot, chip = entry >> 4, entry & 15
        which, k = slot & 3, slot >> 2
        m = 16 * k + chip
        good = slot < all_full[half]
        at = jnp.int32(4 * EARLY)
        for later in range(EARLY, WT):
            for i in range(4):
                has = full[2 * i + half] > later
                hit = (slot == jnp.where(has, at, -1))
                which, k, m = jnp.where(hit, i, which), jnp.where(hit, later, k), jnp.where(hit, 16 * later + chip, m)
                at = at + has.astype(jnp.int32)
        order = 16 * (slot - all_full[half]) + chip
        order = jnp.where(slot >= all_full[half], order, -1)
        for i in range(4):
            h = 2 * i + half
            hit = (order >= start[h]) & (order < start[h] + left[h])
            which, k = jnp.where(hit, i, which), jnp.where(hit, full[h], k)
            m = jnp.where(hit, 16 * full[h] + order - start[h], m)
        good = good | ((order >= 0) & (order < all_left[half]))
        which, k, m = jnp.where(good, which, 0), jnp.where(good, k, 0), jnp.where(good, m, 0)
        wide = 4 * size[half]
        for i in range(1, 4):
            wide = jnp.where(which == i, 4 * size[2 * i + half], jnp.broadcast_to(wide, (8, LANES)))
        position = m * LANES
        quad = ((position.astype(jnp.float32) + 0.5) / wide.astype(jnp.float32)).astype(jnp.int32)
        offset = position - quad * wide
        quad = quad + (2 * which + half) * NQ
        values = [3 * quad + (offset >> 7), 3 * quad + 3, offset & 127, wide - offset,
                  which * 8 + k + jnp.where(good, 64, 0)]
        here = (line >= 3 * half) & (line < 3 * half + 3)
        fields = [jnp.where(here, v, f) for v, f in zip(values, fields)]
    for i in range(FIELDS):
        table[8 * i:8 * i + 8, :] = fields[i]

    def mine(values):
        out = values[0]
        for h in range(1, NIRR):
            out = jnp.where(row == h, values[h], out)
        return out

    my_size, my_live, my_full, my_start = mine(size), mine(live), mine(full), mine(start)
    load_b.wait()
    for q in range(NQ):
        x_b[q, 0:36, :] = b_v[:, q * QUAD:(q + 1) * QUAD].astype(jnp.float32)
    y_b[3 * NQ] = jnp.zeros((40, LANES), jnp.float32)
    packed_b = jnp.dot(
        x_b[...].reshape(NQ * 40, QUAD).astype(jnp.bfloat16), selection(my_size),
        preferred_element_type=jnp.float32)
    for q in range(NQ):
        for t in range(3):
            y_b[3 * q + t] = packed_b[40 * q:40 * q + 40, t * LANES:(t + 1) * LANES]
    lane_b = lax.broadcasted_iota(jnp.int32, (40, LANES), 1)

    @pl.loop(0, 16 * WT // 8, init_carry=(jnp.int32(0), jnp.int32(0)))
    def _(group, carry):
        quad, offset = carry
        for u in range(8):
            m = 8 * group + u
            t = jnp.minimum(3 * quad + offset // LANES, 3 * NQ - 1)
            after = jnp.minimum(3 * quad + 3, 3 * NQ)
            v = moved(y_b[t], y_b[t + 1], y_b[after], lane_b, offset % LANES, 4 * my_size - offset)
            chip = (m + jnp.where(m >= 16 * my_full, my_start, 0)) % 16
            b_pack[chip, m // 16] = jnp.where(lane_b < my_live - m * LANES, v, 0.0).astype(jnp.bfloat16)
            offset = offset + LANES
            over = offset >= 4 * my_size
            quad, offset = jnp.where(over, quad + 1, quad), jnp.where(over, offset - 4 * my_size, offset)
        return quad, offset

    store = pltpu.make_async_copy(b_pack, b_out, s_load)
    store.start()
    store.wait()


def deal_call(sizes, window, integrals):
    bf, f32 = jnp.bfloat16, jnp.float32
    smem = pl.BlockSpec(memory_space=pltpu.SMEM)
    hbm = pl.BlockSpec(memory_space=pl.ANY)
    return pl.pallas_call(
        deal_kernel,
        out_shape=(jax.ShapeDtypeStruct((16, WT, 40, LANES), bf),
                   jax.ShapeDtypeStruct((8 * FIELDS, LANES), jnp.int32), jax.ShapeDtypeStruct((1,), jnp.int32)),
        in_specs=[smem, smem, hbm],
        out_specs=(hbm, pl.BlockSpec(memory_space=pltpu.VMEM), smem),
        scratch_shapes=[
            pltpu.VMEM((36, NB * NB), bf),
            pltpu.VMEM((NQ, 40, QUAD), f32),
            pltpu.VMEM((NQ * 3 + 1, 40, LANES), f32),
            pltpu.VMEM((16, WT, 40, LANES), bf),
            pltpu.SemaphoreType.DMA,
        ],
        compiler_params=pltpu.CompilerParams(vmem_limit_bytes=60 * 2**20),
    )(sizes, window, integrals)


def kernel(kt, table, window, sizes, a_hbm, b_hbm, o_ref,
           a_v, y_a, chosen, a_send, b_first, b_second, dense, a_recv, a_mat, b_main, c_part, c_in1, c_sum, c_in2, c_out,
           s_load, s_bs, s_br, s_as, s_ar, s_zs, s_zr, s_rs, s_rr, s_ks, s_kr, s_c1s, s_c1r, s_c2s, s_c2r):
    row, col = lax.axis_index("row"), lax.axis_index("col")
    x, core = row // 2, row % 2
    z, y = col // 4, col % 4
    chip = x * 4 + y

    def plane(i):
        step = (7 * i) % 16
        px, py = (x + step // 4) % 4, (y + step) % 4
        return (px * 2 + core, z * 4 + py), px * 4 + py

    up = (row, ((z + 1) % 8) * 4 + y)
    down = (row, ((z + 7) % 8) * 4 + y)
    sibling = (x * 2 + 1 - core, col)

    tiles_of = (pl.ds(0, EARLY), pl.ds(EARLY, WT - EARLY))
    b_recv = (b_first, b_second)
    own_b = [pltpu.make_async_copy(b_hbm.at[chip, tiles_of[i]], b_recv[i].at[chip], s_load.at[8 + i]) for i in range(2)]
    for c in own_b:
        c.start()

    def load(h):
        part = pl.ds(pl.multiple_of(h * NB * NB, LANES), NB * NB)
        return pltpu.make_async_copy(a_hbm.at[:, part], a_v.at[:, part], s_load.at[h])

    @pl.loop(0, NIRR)
    def _(h):
        load(h).start()

    barrier = pltpu.get_barrier_semaphore()

    @pl.loop(1, 16)
    def _(i):
        pl.semaphore_signal(barrier, 1, device_id=plane(i)[0], device_id_type=MESH)

    for who in (up, down, sibling):
        pl.semaphore_signal(barrier, 1, device_id=who, device_id_type=MESH)
    pl.semaphore_wait(barrier, 18)

    def remote(src, dst, send, recv, who):
        return pltpu.make_async_remote_copy(src, dst, send, recv, device_id=who, device_id_type=MESH)

    def start(copies):
        for c in copies:
            c.start()
        return copies

    def got(copies):
        for c in copies:
            c.wait_recv()

    def b_copy(chunk, i):
        who, target = plane(i)
        return remote(b_hbm.at[target, tiles_of[chunk]], b_recv[chunk].at[chip], s_bs.at[chunk, i], s_br.at[chunk, i], who)

    for chunk in range(2):
        pl.loop(1, 16)(lambda i: b_copy(chunk, i).start())

    y_a[3 * NIRR * NQ] = jnp.zeros((24, LANES), jnp.float32)

    @pl.loop(0, NIRR)
    def _(h):
        load(h).wait()
        chosen[...] = selection(sizes[h ^ window[0]])

        @pl.loop(0, 3)
        def _(part):
            first = h * NQ + 8 * part
            wide = [a_v[:, pl.ds(pl.multiple_of((first + q) * QUAD, LANES), QUAD)].astype(jnp.float32)
                    for q in range(8)]
            packed = jnp.dot(jnp.concatenate(wide, axis=0).astype(jnp.bfloat16), chosen[...],
                             preferred_element_type=jnp.float32)
            for q in range(8):
                for t in range(3):
                    y_a[(first + q) * 3 + t] = packed[24 * q:24 * q + 24, t * LANES:(t + 1) * LANES]

    lane_a = lax.broadcasted_iota(jnp.int32, (24, LANES), 1)

    def pack_a(half, i, target):
        def one(k):
            line, lane = 3 * half + k // 8, (k % 8) * 16 + target
            t, after, shift, rest = (table[8 * f + line, lane] for f in range(4))
            v = moved(y_a[t], y_a[t + 1], y_a[after], lane_a, shift, rest)
            a_send[half, i, :, tile_at(k)] = v.astype(jnp.bfloat16)

        pl.loop(0, kt, unroll=kt // 2 if kt % 2 == 0 else kt // 3 if kt % 3 == 0 else kt)(one)

    def a_copy(half, i):
        who, target = plane(i)
        return remote(a_send.at[half, i], a_recv.at[half, chip], s_as.at[half, i], s_ar.at[half, i], who)

    def own_a(half):
        return pltpu.make_async_copy(a_send.at[half, 0], a_recv.at[half, chip], s_as.at[half, 0])

    def send_a(half):
        @pl.loop(1, 16)
        def _(i):
            pack_a(half, i, plane(i)[1])
            a_copy(half, i).start()

        pack_a(half, 0, chip)
        own_a(half).start()

    def lay_out(i, piece):
        for py in range(4):
            dense[36 * py:36 * py + 36, :] = piece(py)[0:36, :]
        d = dense[...].astype(jnp.bfloat16)
        b_main[0, core, :, tile_at(i)] = d[0:128]
        b_main[8, core, pl.ds(pl.multiple_of(16 * z, 16), 16), tile_at(i)] = d[128:144]

    def lay_out_first():
        own_b[0].wait()
        pl.loop(1, 16)(lambda i: b_copy(0, i).wait_recv())

        @pl.loop(0, 4 * EARLY)
        def _(i):
            lay_out(i, lambda py: b_first[(i % 4) * 4 + py, i // 4].astype(jnp.float32))

    def lay_out_second():
        own_b[1].wait()
        pl.loop(1, 16)(lambda i: b_copy(1, i).wait_recv())

        @pl.loop(4 * EARLY, kt)
        def _(i):
            code = table[32 + 3 * core + i // 8, (i % 8) * 16 + chip]
            px, k = (code >> 3) & 3, jnp.maximum((code & 7) - EARLY, 0)
            lay_out(i, lambda py: jnp.where(code >= 64, b_second[px * 4 + py, k].astype(jnp.float32), 0.0))

    early = 4 * EARLY
    chunks = (pl.ds(0, early * LANES), pl.ds(early * LANES, (kt - early) * LANES))

    def main_copies(step, chunk):
        rows_up = pl.ds(0, 128) if step < 3 else pl.ds(0, 64)
        rows_down = pl.ds(0, 128) if step < 3 else pl.ds(64, 64)
        a, b = (8 - step) % 8, (7 - step) % 8
        at = chunks[chunk]
        return (remote(b_main.at[a, core, rows_up, at], b_main.at[b, core, rows_up, at],
                       s_zs.at[0, step, chunk], s_zr.at[0, step, chunk], up),
                remote(b_main.at[step, core, rows_down, at], b_main.at[step + 1, core, rows_down, at],
                       s_zs.at[1, step, chunk], s_zr.at[1, step, chunk], down))

    def rest_copies(step):
        at_up = pl.ds(pl.multiple_of(16 * ((z + 8 - step) % 8), 16), 16)
        at_down = pl.ds(pl.multiple_of(16 * ((z + step) % 8), 16), 16)
        out = [remote(b_main.at[8, core, at_up], b_main.at[8, core, at_up], s_rs.at[0, step], s_rr.at[0, step], up)]
        if step < 3:
            out.append(remote(b_main.at[8, core, at_down], b_main.at[8, core, at_down],
                              s_rs.at[1, step], s_rr.at[1, step], down))
        return out

    main, rest = {}, []

    def share(r, chunk):
        at = chunks[chunk]
        return remote(b_main.at[r, core, :, at], b_main.at[r, core, :, at], s_ks.at[r, chunk], s_kr.at[r, chunk], sibling)

    def next_rest(step):
        if step:
            got(rest[step - 1])
        rest.append(start(rest_copies(step)))

    def next_main(step, chunk):
        if step:
            got(main[step - 1, chunk])
        main[step, chunk] = start(main_copies(step, chunk))
        for r in sorted({step, (8 - step) % 8}):
            share(r, chunk).start()

    def repack(half):
        own_a(half).wait()
        pl.loop(1, 16)(lambda i: a_copy(half, i).wait_recv())

        @pl.loop(0, 8)
        def _(s):
            v = a_recv[half, pl.ds(2 * s, 2)].astype(jnp.float32)
            a_mat[half, pl.ds(pl.multiple_of(48 * s, 48), 48), :] = v.reshape(48, kt * LANES).astype(jnp.bfloat16)

    def tile_of(u):
        by_distance = ((u + 1) // 2 * (2 * (u % 2) - 1) + 8) % 8
        return (1 - u // 7) * by_distance + u // 7 * 8 - u // 8 * 4

    def product(r):
        for chunk in range(2):
            share(r, chunk).wait_recv()
        total = None
        for half in range(2):
            v = lax.dot_general(a_mat[half], b_main[r, half], (((1,), (1,)), ((), ())),
                                preferred_element_type=jnp.float32)
            total = v if total is None else total + v
        total = total.reshape(4, 4, 24, LANES)
        odd = r % 2
        for i in range(4):
            for j in range(4):
                c_part[r, i + odd * (j - i), j + odd * (i - j)] = total[i, j]

    def line_peer(r, k, odd):
        return (((x + k * (1 - odd)) % 4) * 2 + core, z * 4 + (y + k * odd) % 4)

    def first_copies(r):
        odd = r % 2
        mine = x + odd * (y - x)
        return [remote(c_part.at[r, (mine + k) % 4], c_in1.at[r, k - 1], s_c1s.at[r, k - 1], s_c1r.at[r, k - 1],
                       line_peer(r, k, odd)) for k in (1, 3, 2)]

    def second_copies(r):
        odd = r % 2
        mine = y + odd * (x - y)
        return [remote(c_sum.at[r, (mine + k) % 4], c_in2.at[r, k - 1], s_c2s.at[r, k - 1], s_c2r.at[r, k - 1],
                       line_peer(r, k, 1 - odd)) for k in (1, 3, 2)]

    def send_second(r):
        got(first_copies(r))
        c_sum[r] = c_part[r, x + r % 2 * (y - x)] + c_in1[r, 0] + c_in1[r, 1] + c_in1[r, 2]
        start(second_copies(r))

    def finish(r):
        got(second_copies(r))
        total = c_sum[r, y + r % 2 * (x - y)] + c_in2[r, 0] + c_in2[r, 1] + c_in2[r, 2]
        c_out[r // 8 * 8 + (1 - r // 8) * ((z + r) % 8)] = total

    send_a(0)
    lay_out_first()
    next_main(0, 0)
    send_a(1)
    lay_out_second()
    next_main(0, 1)
    next_rest(0)
    next_main(1, 0)
    next_rest(1)
    next_main(1, 1)
    next_rest(2)
    next_main(2, 0)
    next_rest(3)
    next_main(2, 1)
    repack(0)
    next_main(3, 0)
    got(rest[3])
    for chunk in range(2):
        share(8, chunk).start()
    next_main(3, 1)
    repack(1)

    @pl.loop(0, 13)
    def _(u):
        @pl.when(u == 8)
        def _():
            for chunk in range(2):
                got(main[3, chunk])
                share(4, chunk).start()

        @pl.when(u < 9)
        def _():
            r = tile_of(u)
            product(r)
            start(first_copies(r))

        @pl.when((u >= 2) & (u < 11))
        def _():
            send_second(tile_of(u - 2))

        @pl.when(u >= 4)
        def _():
            finish(tile_of(u - 4))

    size_b = jnp.int32(0)
    for h in range(NIRR):
        size_b = jnp.where(window[1] == h, sizes[h], size_b)
    for t in range(8):
        o_ref[:, 144 * t:144 * t + 128] = c_out[t]
        o_ref[:, 144 * t + 128:144 * t + 144] = c_out[8, :, 16 * t:16 * t + 16]
    slot = lax.broadcasted_iota(jnp.int32, (24, 8 * 144), 1)
    o_ref[...] = jnp.where(slot % NB < size_b, o_ref[...], 0.0)

    @pl.loop(1, 16)
    def _(i):
        for half in range(2):
            a_copy(half, i).wait_send()
            b_copy(half, i).wait_send()

    @pl.loop(0, 9)
    def _(r):
        for c in first_copies(r) + second_copies(r) + [share(r, 0), share(r, 1)]:
            c.wait_send()

    for copies in rest + list(main.values()):
        for c in copies:
            c.wait_send()


def ladder_call(kt, collective_id, table, window, sizes, amplitudes, b_packed):
    kh = kt * LANES
    bf, f32 = jnp.bfloat16, jnp.float32
    dma = pltpu.SemaphoreType.DMA
    smem = pl.BlockSpec(memory_space=pltpu.SMEM)
    hbm = pl.BlockSpec(memory_space=pl.ANY)
    return pl.pallas_call(
        functools.partial(kernel, kt),
        out_shape=jax.ShapeDtypeStruct((24, 8 * 144), f32),
        in_specs=[smem] * 3 + [hbm] * 2,
        out_specs=pl.BlockSpec(memory_space=pltpu.VMEM),
        scratch_shapes=[
            pltpu.VMEM((24, NIRR * NB * NB), bf),
            pltpu.VMEM((NIRR * NQ * 3 + 1, 24, LANES), f32),
            pltpu.VMEM((QUAD, QUAD), bf),
            pltpu.VMEM((2, 16, 24, kh), bf),
            pltpu.VMEM((16, EARLY, 40, LANES), bf),
            pltpu.VMEM((16, WT - EARLY, 40, LANES), bf),
            pltpu.VMEM((144, LANES), f32),
            pltpu.VMEM((2, 16, 24, kh), bf),
            pltpu.VMEM((2, 384, kh), bf),
            pltpu.VMEM((9, 2, 128, kh), bf),
            pltpu.VMEM((9, 4, 4, 24, LANES), f32),
            pltpu.VMEM((9, 3, 4, 24, LANES), f32),
            pltpu.VMEM((9, 4, 24, LANES), f32),
            pltpu.VMEM((9, 3, 24, LANES), f32),
            pltpu.VMEM((9, 24, LANES), f32),
            dma((10,)), dma((2, 16)), dma((2, 16)), dma((2, 16)), dma((2, 16)),
            dma((2, 4, 2)), dma((2, 4, 2)), dma((2, 4)), dma((2, 4)), dma((9, 2)), dma((9, 2)),
            dma((9, 3)), dma((9, 3)), dma((9, 3)), dma((9, 3)),
        ],
        compiler_params=pltpu.CompilerParams(
            collective_id=collective_id, has_side_effects=True, vmem_limit_bytes=60 * 2**20),
    )(table, window, sizes, amplitudes, b_packed)


def shards(amplitudes, integrals, block_sizes, window_irreps):
    b_packed, table, width = deal_call(block_sizes, window_irreps, integrals)
    which = sum((width[0] > w).astype(jnp.int32) for w in WIDTHS[:-1])
    calls = [functools.partial(ladder_call, w, i) for i, w in enumerate(WIDTHS)]
    return lax.switch(which, calls, table, window_irreps, block_sizes, amplitudes, b_packed)


def solution(mesh):
    placed = (P(("row", "col"), None), P("col", "row"), P(), P())
    return jax.shard_map(
        shards, mesh=mesh, in_specs=placed, out_specs=P(("row", "col"), None), check_vma=False
    )
```

time: 263 us -> 93.8 us (0.36)
  waiting for transfers between devices: 193 us -> 0 us
  Pallas kernels: 0 us -> 90.8 us
  local copies, waits for them, and re-layouts: 26.6 us -> 0.65 us
  matrix products: 12.1 us -> 0 us
  between operations: 13.4 us -> 1.96 us
  other arithmetic: 7.95 us -> 0 us
  starting transfers between devices: 6.94 us -> 0 us
    all_gather x1 -> x0, waiting for transfers between devices: 126 us -> none  [shards(): lax.all_gather(integrals, 'col', axis=0, tiled=True)]
    pallas_call x0 -> x2, Pallas kernels: none -> 90.8 us  [the longest x1 86 us: ladder_call(): pl.pallas_call(functools.partial(kernel, kt), out_shape=jax.ShapeDtypeStr...]
    all_to_all x1 -> x0, waiting for transfers between devices: 39.5 us -> none  [shards(): lax.all_to_all(amplitudes, 'row', split_axis=1, concat_axis=0, tiled=True)]
    unnamed x3 -> x0, waiting for transfers between devices: 28.1 us -> none
    unnamed x7 -> x1, local copies, waits for them, and re-layouts: 22 us -> 0.65 us
    dot_general x1 -> x0, matrix products: 12.1 us -> none  [contract(): lax.dot_general(left_rows, right_rows, (((1,), (1,)), ((), ())), preferre...]
    all_to_all x1 -> x0, starting transfers between devices: 6.94 us -> none  [shards(): lax.all_to_all(amplitudes, 'row', split_axis=1, concat_axis=0, tiled=True)]
    all_to_all x1 -> x0, local copies, waits for them, and re-layouts: 4.05 us -> none  [shards(): lax.all_to_all(amplitudes, 'row', split_axis=1, concat_axis=0, tiled=True)]
  transfers between devices with their start and end apart: 3 -> 0, of which waited for: 3 -> 0; matrix products, arithmetic and copies ran while one was open for 4% -> 0% of each run, Pallas kernels for 0% -> 0%
where the time goes in v2:
time: 93.8 us; the launch traced here: 93.6 us
  Pallas kernels  90.8 us (97%)
  between operations  1.96 us (2%)
    pallas_call x1, Pallas kernels, ladder_call(): pl.pallas_call(functools.partial(kernel, kt), out_shape=jax.ShapeDtypeStr...  86 us
    pallas_call x1, Pallas kernels, deal_call(): pl.pallas_call(deal_kernel, out_shape=(jax.ShapeDtypeStruct((16, WT, 40,...  4.76 us

profile of v2, /device:TPU:1, one launch (start us, length us, event | category | flops | bytes accessed | tf_op | source)
XLA Modules:
  0.0 93.6 jit_solution(1213782852087674978)
XLA Ops:
  0.0 4.8 %shard_map.54 = (bf16[16,5,40,128]{3,2,1,0:T(8,128)(2,1)S(1)}, s32[40,128]{1,0:T(8,128)S(1)}, s32[1]{0:T(128)}) custom-call(s32[8]{0:T(128)} %sizes.1, s32[2]{0:T(128)} %window.1, bf16[36,9216]{1,0:T(8,128)(2,1)} %b_hbm.1), custom_call_target="tpu_custom_call" | custom-call | tf_op jit(solution)/shard_map/pallas_call | solution.py:141
  6.7 86.3 %conditional.1 = (f32[24,1152]{1,0:T(8,128)S(1)}) conditional(s32[]{:T(128)} %bitcast, (s32[40,128]{1,0:T(8,128)S(1)}, s32[2]{0:T(128)}, s32[8]{0:T(128)}, bf16[24,73728]{1,0:T(8,128)(2,1)}, bf16[16,5,40,128]{3,2,1,0:T(8,128)(2,1)S(1)}) %tuple.17, (s32[40,128]{1,0:T(8,128)S(1)}, s32[2]{0:T(128)}, s32[8]{0:T(128)}, ...), branch_computations={%region_0.0_spmd, %region_1.0_spmd, %region_2.0_spmd, %region_3.0_... | conditional | bytes 8 | solution.py:489
  6.7 86.0 %branch_1_fun.1 = f32[24,1152]{1,0:T(8,128)S(1)} custom-call(s32[40,128]{1,0:T(8,128)S(1)} %get-tuple-element.55.table, s32[2]{0:T(128)} %get-tuple-element.56.window, s32[8]{0:T(128)} %get-tuple-element.57.sizes, bf16[24,73728]{1,0:T(8,128)(2,1)} %get-tuple-element.82.a_hbm, bf16[16,5,40,128]{3,2,1,0:T(8,128)(2,1)S(1)} %get-tuple-element.59.b_hbm), custom_call_target="tpu_custom_call" | custom-call | tf_op jit(solution)/shard_map/cond/branch_1_fun/pallas_call | solution.py:455
  93.0 0.6 copy.18

commit v3 on v2

--- a/solution.py
+++ b/solution.py
@@ -87,7 +87,7 @@
         position = m * LANES
         quad = ((position.astype(jnp.float32) + 0.5) / wide.astype(jnp.float32)).astype(jnp.int32)
         offset = position - quad * wide
-        quad = quad + (2 * which + half) * NQ
+        quad = quad + (which + 4 * half) * NQ
         values = [3 * quad + (offset >> 7), 3 * quad + 3, offset & 127, wide - offset,
                   which * 8 + k + jnp.where(good, 64, 0)]
         here = (line >= 3 * half) & (line < 3 * half + 3)
@@ -183,8 +183,8 @@
         return pltpu.make_async_copy(a_hbm.at[:, part], a_v.at[:, part], s_load.at[h])
 
     @pl.loop(0, NIRR)
-    def _(h):
-        load(h).start()
+    def _(i):
+        load(2 * (i % 4) + i // 4).start()
 
     barrier = pltpu.get_barrier_semaphore()
 
@@ -215,23 +215,27 @@
     for chunk in range(2):
         pl.loop(1, 16)(lambda i: b_copy(chunk, i).start())
 
-    y_a[3 * NIRR * NQ] = jnp.zeros((24, LANES), jnp.float32)
-
-    @pl.loop(0, NIRR)
-    def _(h):
-        load(h).wait()
-        chosen[...] = selection(sizes[h ^ window[0]])
-
-        @pl.loop(0, 3)
-        def _(part):
-            first = h * NQ + 8 * part
-            wide = [a_v[:, pl.ds(pl.multiple_of((first + q) * QUAD, LANES), QUAD)].astype(jnp.float32)
-                    for q in range(8)]
-            packed = jnp.dot(jnp.concatenate(wide, axis=0).astype(jnp.bfloat16), chosen[...],
-                             preferred_element_type=jnp.float32)
-            for q in range(8):
-                for t in range(3):
-                    y_a[(first + q) * 3 + t] = packed[24 * q:24 * q + 24, t * LANES:(t + 1) * LANES]
+    for half in range(2):
+        y_a[12 * NQ * (half + 1)] = jnp.zeros((24, LANES), jnp.float32)
+
+    def pack_quads(half):
+        @pl.loop(0, 4)
+        def _(i):
+            h = 2 * i + half
+            load(h).wait()
+            chosen[...] = selection(sizes[h ^ window[0]])
+
+            @pl.loop(0, 3)
+            def _(part):
+                first = h * NQ + 8 * part
+                to = (4 * half + i) * NQ + 8 * part
+                wide = [a_v[:, pl.ds(pl.multiple_of((first + q) * QUAD, LANES), QUAD)].astype(jnp.float32)
+                        for q in range(8)]
+                packed = jnp.dot(jnp.concatenate(wide, axis=0).astype(jnp.bfloat16), chosen[...],
+                                 preferred_element_type=jnp.float32)
+                for q in range(8):
+                    for t in range(3):
+                        y_a[(to + q) * 3 + t] = packed[24 * q:24 * q + 24, t * LANES:(t + 1) * LANES]
 
     lane_a = lax.broadcasted_iota(jnp.int32, (24, LANES), 1)
 
@@ -334,23 +338,30 @@
             v = a_recv[half, pl.ds(2 * s, 2)].astype(jnp.float32)
             a_mat[half, pl.ds(pl.multiple_of(48 * s, 48), 48), :] = v.reshape(48, kt * LANES).astype(jnp.bfloat16)
 
-    def tile_of(u):
-        by_distance = ((u + 1) // 2 * (2 * (u % 2) - 1) + 8) % 8
-        return (1 - u // 7) * by_distance + u // 7 * 8 - u // 8 * 4
-
-    def product(r):
+    def arrived(r):
         for chunk in range(2):
             share(r, chunk).wait_recv()
+
+    def product(v, halves):
         total = None
-        for half in range(2):
-            v = lax.dot_general(a_mat[half], b_main[r, half], (((1,), (1,)), ((), ())),
-                                preferred_element_type=jnp.float32)
-            total = v if total is None else total + v
-        total = total.reshape(4, 4, 24, LANES)
-        odd = r % 2
-        for i in range(4):
-            for j in range(4):
-                c_part[r, i + odd * (j - i), j + odd * (i - j)] = total[i, j]
+        for half in halves:
+            both = jnp.concatenate([b_main[v, half], b_main[8 - v, half]], axis=0)
+            part = lax.dot_general(a_mat[half], both, (((1,), (1,)), ((), ())), preferred_element_type=jnp.float32)
+            total = part if total is None else total + part
+        for n, r in enumerate((v, 8 - v)):
+            tile = total[:, n * LANES:(n + 1) * LANES].reshape(4, 4, 24, LANES)
+            odd = r % 2
+            for i in range(4):
+                for j in range(4):
+                    a, b = i + odd * (j - i), j + odd * (i - j)
+                    c_part[r, a, b] = c_part[r, a, b] + tile[i, j] if halves == (1,) else tile[i, j]
+
+    def for_pair(v, act):
+        act(v)
+
+        @pl.when(v < 4)
+        def _():
+            act(8 - v)
 
     def line_peer(r, k, odd):
         return (((x + k * (1 - odd)) % 4) * 2 + core, z * 4 + (y + k * odd) % 4)
@@ -377,9 +388,11 @@
         total = c_sum[r, y + r % 2 * (x - y)] + c_in2[r, 0] + c_in2[r, 1] + c_in2[r, 2]
         c_out[r // 8 * 8 + (1 - r // 8) * ((z + r) % 8)] = total
 
+    pack_quads(0)
     send_a(0)
     lay_out_first()
     next_main(0, 0)
+    pack_quads(1)
     send_a(1)
     lay_out_second()
     next_main(0, 1)
@@ -391,35 +404,48 @@
     next_main(2, 0)
     next_rest(3)
     next_main(2, 1)
-    repack(0)
-    next_main(3, 0)
     got(rest[3])
     for chunk in range(2):
         share(8, chunk).start()
+    repack(0)
+
+    @pl.loop(0, 3)
+    def _(v):
+        for_pair(v, arrived)
+        product(v, (0,))
+
+    next_main(3, 0)
     next_main(3, 1)
     repack(1)
 
-    @pl.loop(0, 13)
-    def _(u):
-        @pl.when(u == 8)
+    @pl.loop(0, 7)
+    def _(v):
+        @pl.when(v == 4)
         def _():
             for chunk in range(2):
                 got(main[3, chunk])
                 share(4, chunk).start()
 
-        @pl.when(u < 9)
-        def _():
-            r = tile_of(u)
-            product(r)
-            start(first_copies(r))
-
-        @pl.when((u >= 2) & (u < 11))
-        def _():
-            send_second(tile_of(u - 2))
-
-        @pl.when(u >= 4)
-        def _():
-            finish(tile_of(u - 4))
+        @pl.when(v < 3)
+        def _():
+            product(v, (1,))
+
+        @pl.when((v >= 3) & (v < 5))
+        def _():
+            for_pair(v, arrived)
+            product(v, (0, 1))
+
+        @pl.when(v < 5)
+        def _():
+            for_pair(v, lambda r: start(first_copies(r)))
+
+        @pl.when((v >= 1) & (v < 6))
+        def _():
+            for_pair(v - 1, send_second)
+
+        @pl.when(v >= 2)
+        def _():
+            for_pair(v - 2, finish)
 
     size_b = jnp.int32(0)
     for h in range(NIRR):

time: 93.8 us -> 92.9 us (level)
  no operation moved by 1% of the time
where the time goes in v3:
time: 92.9 us; the launch traced here: 92.8 us
  Pallas kernels  89.9 us (97%)
  between operations  1.96 us (2%)
    pallas_call x1, Pallas kernels, ladder_call(): pl.pallas_call(functools.partial(kernel, kt), out_shape=jax.ShapeDtypeStr...  85.1 us
    pallas_call x1, Pallas kernels, deal_call(): pl.pallas_call(deal_kernel, out_shape=(jax.ShapeDtypeStruct((16, WT, 40,...  4.76 us

profile of v3, /device:TPU:1, one launch (start us, length us, event | category | flops | bytes accessed | tf_op | source)
XLA Modules:
  0.0 92.8 jit_solution(7207731624186923)
XLA Ops:
  0.0 4.8 %shard_map.54 = (bf16[16,5,40,128]{3,2,1,0:T(8,128)(2,1)S(1)}, s32[40,128]{1,0:T(8,128)S(1)}, s32[1]{0:T(128)}) custom-call(s32[8]{0:T(128)} %sizes.1, s32[2]{0:T(128)} %window.1, bf16[36,9216]{1,0:T(8,128)(2,1)} %b_hbm.1), custom_call_target="tpu_custom_call" | custom-call | tf_op jit(solution)/shard_map/pallas_call | solution.py:141
  6.7 85.4 %conditional.1 = (f32[24,1152]{1,0:T(8,128)S(1)}) conditional(s32[]{:T(128)} %bitcast, (s32[40,128]{1,0:T(8,128)S(1)}, s32[2]{0:T(128)}, s32[8]{0:T(128)}, bf16[24,73728]{1,0:T(8,128)(2,1)}, bf16[16,5,40,128]{3,2,1,0:T(8,128)(2,1)S(1)}) %tuple.17, (s32[40,128]{1,0:T(8,128)S(1)}, s32[2]{0:T(128)}, s32[8]{0:T(128)}, ...), branch_computations={%region_0.0_spmd, %region_1.0_spmd, %region_2.0_spmd, %region_3.0_... | conditional | bytes 8 | solution.py:515
  6.7 85.1 %branch_0_fun.1 = f32[24,1152]{1,0:T(8,128)S(1)} custom-call(s32[40,128]{1,0:T(8,128)S(1)} %get-tuple-element.48.table, s32[2]{0:T(128)} %get-tuple-element.50.window, s32[8]{0:T(128)} %get-tuple-element.52.sizes, bf16[24,73728]{1,0:T(8,128)(2,1)} %get-tuple-element.81.a_hbm, bf16[16,5,40,128]{3,2,1,0:T(8,128)(2,1)S(1)} %get-tuple-element.54.b_hbm), custom_call_target="tpu_custom_call" | custom-call | tf_op jit(solution)/shard_map/cond/branch_0_fun/pallas_call | solution.py:481
  92.1 0.6 copy.18
